TPU v7x, 512 devices: a whole 4x8x8 slice. The times are simulated.
512 devices in a mesh: seq: 64 (over y, x, core), tp: 8 (over z).
Axes of the slice: x: 4, y: 8, z: 8, core: 2. Of those that a mesh axis runs over, the one named last changes fastest.
Arguments:
- queries: bfloat16 [32768, 4096], P('seq', 'tp'), may hold values from -9 to 9
- keys: bfloat16 [32768, 4096], P('seq', 'tp'), may hold values from -9 to 9
- values: bfloat16 [32768, 4096], P('seq', 'tp'), may hold values from -6 to 6
- route: int32 [32, 32768], P('tp', 'seq'), may hold values from 0 to 32767, as said below
- members: int32 [32, 32768], P('tp', 'seq'), may hold values from 0 to 32767, as said below
- pattern: int32 [32, 128, 10], P('tp', 'seq'), may hold values from 0 to 1, as said below
- w_out: bfloat16 [4096, 4096], P('tp', 'seq'), may hold values from -0.25 to 0.25
Outputs:
- mixed: bfloat16 [32768, 4096], P('seq', 'tp')
Inputs may be any that keep to these rules, and one draw needn't show every extreme that they name: `route`: each row is a permutation of the positions; for every aligned block of 512 positions and every aligned block of 512 slots, exactly 8 of the block's positions have their slot in that slot block. members[h] is the inverse permutation of route[h]: members[h, route[h, p]] = p. `pattern`: entries 2 * 2 and 2 * 2 + 1 (the cluster's own blocks) are always 1; entries whose cluster lies outside 0 to 127 are always 0.
All inputs are finite; a program needn't handle non-finite values.
Results may differ from a plain program's by a relative error of at most 0.017.
Values may be sent and summed in bfloat16 or wider, within the bound.
A program may use at most 64 MiB of HBM per device.

v0:
```python
import jax
import jax.numpy as jnp
from jax import lax
from jax.sharding import PartitionSpec as P

CLUSTER = 256
REACH = 2


def extended_2(cells, sides, width):
    for axis, dim in sides:
        count = lax.axis_size(axis)
        ends = count - 1
        head = lax.slice_in_dim(cells, 0, width, axis=dim)
        tail = lax.slice_in_dim(cells, cells.shape[dim] - width, cells.shape[dim], axis=dim)
        cells = jnp.concatenate(
            [
                lax.ppermute(tail, axis, [(i, (i + 1) % count) for i in range(ends)]),
                cells,
                lax.ppermute(head, axis, [((i + 1) % count, i) for i in range(ends)]),
            ],
            axis=dim,
        )
    return cells


def attend_head(pieces):
    query_rows, key_rows, value_rows, pattern_rows = pieces
    head_width = query_rows.shape[1]
    cluster_count = query_rows.shape[0] // CLUSTER
    window_rows = (2 * REACH + 1) * CLUSTER
    starts = jnp.arange(cluster_count) * CLUSTER
    key_window = jax.vmap(
        lambda slot_start: lax.dynamic_slice_in_dim(key_rows, slot_start, window_rows, 0)
    )(starts)
    value_window = jax.vmap(
        lambda slot_start: lax.dynamic_slice_in_dim(value_rows, slot_start, window_rows, 0)
    )(starts)
    query_blocks = query_rows.reshape(cluster_count, CLUSTER, head_width)
    scores = jnp.einsum(
        "cqd,ckd->cqk", query_blocks, key_window, preferred_element_type=jnp.float32
    ) * head_width ** (-0.5)
    allowed = jnp.repeat(pattern_rows, CLUSTER // 2, axis=1) > 0
    scores = jnp.where(allowed[:, None, :], scores, -jnp.inf)
    row_max = jnp.max(scores, axis=-1, keepdims=True)
    exponent = jnp.exp(scores - row_max)
    weights = (exponent / jnp.sum(exponent, axis=-1, keepdims=True)).astype(jnp.bfloat16)
    context = jnp.einsum(
        "cqk,ckd->cqd", weights, value_window, preferred_element_type=jnp.float32
    ).astype(jnp.bfloat16)
    return context.reshape(query_rows.shape[0], head_width)


def buffer_index(group_of, order_key, per_peer):
    same_group = group_of[:, :, None] == group_of[:, None, :]
    earlier = order_key[:, None, :] < order_key[:, :, None]
    rank = jnp.sum((same_group & earlier).astype(jnp.int32), axis=2)
    return group_of * per_peer + rank


def shards(queries, keys, values, route, members, pattern, w_out):
    rows_here = queries.shape[0]
    head_count = route.shape[0]
    head_width = queries.shape[1] // head_count
    peer_count = lax.axis_size("seq")
    per_peer = rows_here // peer_count
    local_iota = jnp.arange(rows_here, dtype=jnp.int32)
    send_index = buffer_index(route // rows_here, route, per_peer)
    local_slots = jnp.broadcast_to(local_iota[None, :], members.shape)
    arrival_index = buffer_index(members // rows_here, local_slots, per_peer)
    send_table = (send_index[:, None, :] == local_iota[None, :, None]).astype(jnp.bfloat16)
    land_table = (arrival_index[:, :, None] == local_iota[None, None, :]).astype(jnp.bfloat16)
    stacked = jnp.concatenate(
        [
            queries.reshape(rows_here, head_count, head_width),
            keys.reshape(rows_here, head_count, head_width),
            values.reshape(rows_here, head_count, head_width),
        ],
        axis=2,
    )
    packed = jnp.einsum(
        "hap,phd->had", send_table, stacked, preferred_element_type=jnp.float32
    ).astype(jnp.bfloat16)

    def outgoing(column_index):
        part_rows = packed[:, :, column_index * head_width : (column_index + 1) * head_width]
        return part_rows.reshape(head_count, peer_count, per_peer, head_width)

    sent_query, sent_key, sent_value = (
        lax.all_to_all(outgoing(0), "seq", split_axis=1, concat_axis=1, tiled=True),
        lax.all_to_all(outgoing(1), "seq", split_axis=1, concat_axis=1, tiled=True),
        lax.all_to_all(outgoing(2), "seq", split_axis=1, concat_axis=1, tiled=True),
    )
    arrived = jnp.concatenate(
        [
            sent_query.reshape(head_count, rows_here, head_width),
            sent_key.reshape(head_count, rows_here, head_width),
            sent_value.reshape(head_count, rows_here, head_width),
        ],
        axis=2,
    )
    placed = jnp.einsum(
        "hsa,had->hsd", land_table, arrived, preferred_element_type=jnp.float32
    ).astype(jnp.bfloat16)
    ordered_query = placed[:, :, :head_width]
    keys_values = jnp.stack(
        [placed[:, :, head_width : 2 * head_width], placed[:, :, 2 * head_width :]]
    )
    extended = extended_2(keys_values, (("seq", 2),), REACH * CLUSTER)
    context = lax.map(attend_head, (ordered_query, extended[0], extended[1], pattern))
    returning = jnp.einsum(
        "hsa,hsd->had", land_table, context, preferred_element_type=jnp.float32
    ).astype(jnp.bfloat16)
    returning = returning.reshape(head_count, peer_count, per_peer, head_width)
    returned = lax.all_to_all(returning, "seq", split_axis=1, concat_axis=1, tiled=True).reshape(
        head_count, rows_here, head_width
    )
    attended = jnp.einsum(
        "hap,had->phd", send_table, returned, preferred_element_type=jnp.float32
    ).astype(jnp.bfloat16)
    attended = attended.reshape(rows_here, head_count * head_width)
    partial_value = jnp.dot(
        attended,
        lax.all_gather(w_out, "seq", axis=1, tiled=True),
        preferred_element_type=jnp.float32,
    )
    column_count = partial_value.shape[1] // lax.axis_size("tp")
    summed = lax.psum(partial_value.astype(jnp.bfloat16), "tp").astype(jnp.float32)
    mixed_out = lax.dynamic_slice_in_dim(
        summed, lax.axis_index("tp") * column_count, column_count, 1
    )
    return mixed_out.astype(jnp.bfloat16)


def solution(mesh):
    placed = (
        P("seq", "tp"),
        P("seq", "tp"),
        P("seq", "tp"),
        P("tp", "seq"),
        P("tp", "seq"),
        P("tp", "seq", None),
        P("tp", "seq"),
    )
    return jax.shard_map(
        shards, mesh=mesh, in_specs=placed, out_specs=P("seq", "tp"), check_vma=False
    )
```

profile of v0, /device:TPU:1, one launch (start us, length us, event | category | flops | bytes accessed | tf_op | source)
XLA Modules:
  0.0 320.6 jit_solution(11738363935786757012)
XLA Ops:
  7.3 1.8 convert_reduce_fusion
  16.0 11.6 %all-to-all-start.2 = ((bf16[4,64,8,128]{3,2,0,1:T(8,128)(2,1)}), bf16[4,64,8,128]{3,2,0,1:T(8,128)(2,1)S(1)}, u32[]{:S(2)}, u32[]{:S(2)}) async-start(bf16[4,64,8,128]{3,2,0,1:T(8,128)(2,1)} %copy.44), calls=%async_computation.2 | async-start | bytes 1048576 | tf_op jit(solution)/shard_map/all_to_all | solution.py:92
  28.5 16.8 %all-to-all-done.2 = bf16[4,64,8,128]{3,2,0,1:T(8,128)(2,1)S(1)} async-done(((bf16[4,64,8,128]{3,2,0,1:T(8,128)(2,1)}), bf16[4,64,8,128]{3,2,0,1:T(8,128)(2,1)S(1)}, u32[]{:S(2)}, u32[]{:S(2)}) %all-to-all-start.2) | async-done | bytes 524320 | tf_op jit(solution)/shard_map/all_to_all | solution.py:92
  45.3 5.7 %all-to-all-start.1 = ((bf16[4,64,8,128]{3,2,0,1:T(8,128)(2,1)}), bf16[4,64,8,128]{3,2,0,1:T(8,128)(2,1)S(1)}, u32[]{:S(2)}, u32[]{:S(2)}) async-start(bf16[4,64,8,128]{3,2,0,1:T(8,128)(2,1)} %copy.42), calls=%async_computation.1 | async-start | bytes 1048576 | tf_op jit(solution)/shard_map/all_to_all | solution.py:91
  51.9 16.8 %all-to-all-done.1 = bf16[4,64,8,128]{3,2,0,1:T(8,128)(2,1)S(1)} async-done(((bf16[4,64,8,128]{3,2,0,1:T(8,128)(2,1)}), bf16[4,64,8,128]{3,2,0,1:T(8,128)(2,1)S(1)}, u32[]{:S(2)}, u32[]{:S(2)}) %all-to-all-start.1) | async-done | bytes 524320 | tf_op jit(solution)/shard_map/all_to_all | solution.py:91
  68.8 5.7 %all-to-all-start = ((bf16[4,64,8,128]{3,2,0,1:T(8,128)(2,1)}), bf16[4,64,8,128]{3,2,0,1:T(8,128)(2,1)S(1)}, u32[]{:S(2)}, u32[]{:S(2)}) async-start(bf16[4,64,8,128]{3,2,0,1:T(8,128)(2,1)} %copy.40), calls=%async_computation | async-start | bytes 1048576 | tf_op jit(solution)/shard_map/all_to_all | solution.py:90
  76.1 16.1 %all-to-all-done = bf16[4,64,8,128]{3,2,0,1:T(8,128)(2,1)S(1)} async-done(((bf16[4,64,8,128]{3,2,0,1:T(8,128)(2,1)}), bf16[4,64,8,128]{3,2,0,1:T(8,128)(2,1)S(1)}, u32[]{:S(2)}, u32[]{:S(2)}) %all-to-all-start) | async-done | bytes 524320 | tf_op jit(solution)/shard_map/all_to_all | solution.py:90
  94.9 3.4 %collective-permute-start = (bf16[2,4,512,128]{3,2,1,0:T(8,128)(2,1)S(1)}, bf16[2,4,512,128]{3,2,1,0:T(8,128)(2,1)S(1)}, u32[]{:S(2)}, u32[]{:S(2)}) collective-permute-start(bf16[2,4,512,128]{3,2,1,0:T(8,128)(2,1)S(1)} %pad_maximum_fusion.1), channel_id=1, source_target_pairs={{0,8},{8,16},{16,24},{24,32},{32,40},{40,48},{48,56},{56,64},{64,7... | collective-permute-start | bytes 3145736 | tf_op jit(solution)/shard_map/ppermute | solution.py:18
  98.3 1.9 collective-permute-start.1
  100.5 9.5 %collective-permute-done = bf16[2,4,512,128]{3,2,1,0:T(8,128)(2,1)S(1)} collective-permute-done((bf16[2,4,512,128]{3,2,1,0:T(8,128)(2,1)S(1)}, bf16[2,4,512,128]{3,2,1,0:T(8,128)(2,1)S(1)}, u32[]{:S(2)}, u32[]{:S(2)}) %collective-permute-start) | collective-permute-done | bytes 1048608 | tf_op jit(solution)/shard_map/ppermute | solution.py:18
  110.0 4.5 %collective-permute-done.1 = bf16[2,4,512,128]{3,2,1,0:T(8,128)(2,1)} collective-permute-done((bf16[2,4,512,128]{3,2,1,0:T(8,128)(2,1)S(1)}, bf16[2,4,512,128]{3,2,1,0:T(8,128)(2,1)}, u32[]{:S(2)}, u32[]{:S(2)}) %collective-permute-start.1) | collective-permute-done | bytes 1048608 | tf_op jit(solution)/shard_map/ppermute | solution.py:20
  114.5 1.3 pad_maximum_fusion
  115.8 1.4 slice_bitcast_fusion
  117.2 27.3 %while.16 = (s32[]{:T(128)}, bf16[4,512,128]{2,1,0:T(8,128)(2,1)}, s32[4,2,10]{2,1,0:T(2,128)}, bf16[4,512,128]{2,1,0:T(8,128)(2,1)}, bf16[4,1536,128]{2,1,0:T(8...) while((s32[]{:T(128)}, bf16[4,512,128]{2,1,0:T(8,128)(2,1)}, ...), condition=%wide.region_5.6_spmd, body=%wide.region_2.5_spmd.sunk | while | flops 509283360 | bytes 7096867 | solution.py:110
  122.0 1.4 fusion.66
  128.8 1.4 fusion.66
  135.6 1.4 fusion.66
  142.4 1.4 fusion.66
  144.5 1.8 fusion.35
  146.5 31.2 %all_to_all.20 = bf16[4,64,8,128]{3,2,0,1:T(8,128)(2,1)S(1)} all-to-all(bf16[4,64,8,128]{3,2,0,1:T(8,128)(2,1)S(1)} %copy.47), channel_id=1, replica_groups=mesh['seq'=64,'tp'=8] {'seq'}, dimensions={1} | all-to-all | bytes 1048576 | tf_op jit(solution)/shard_map/all_to_all | solution.py:115
  178.6 11.8 %all-gather.2.cloned.1.call-done = bf16[512,4096]{0,1:T(8,128)(2,1)} async-done(((bf16[512,64]{0,1:T(8,128)(2,1)}), bf16[512,4096]{0,1:T(8,128)(2,1)}) %all-gather.2.cloned.1.call-update) | async-done | bytes 4194320 | tf_op jit(solution)/shard_map/all_gather | solution.py:124
  190.3 6.6 %convolution_convert_fusion = bf16[512,4096]{1,0:T(8,128)(2,1)} fusion(bf16[512,512]{0,1:T(8,128)(2,1)S(1)} %bitcast.112, bf16[512,4096]{0,1:T(8,128)(2,1)} %all-gather.2.cloned.1.call-done), kind=kOutput, calls=%fused_computation.26 | convolution fusion | flops 2149580800 | bytes 8912896 | tf_op jit(solution)/shard_map/dot_general | solution.py:122
  196.9 115.0 %all-reduce.3.cloned.1.call-done = bf16[512,4096]{1,0:T(8,128)(2,1)} async-done(((bf16[512,4096]{1,0:T(8,128)(2,1)}), bf16[512,4096]{1,0:T(8,128)(2,1)}) %all-reduce.3.cloned.1.call-update) | async-done | bytes 4194320 | tf_op jit(solution)/shard_map/psum | solution.py:128
  311.9 1.9 convert_convert_fusion
  (118 shorter events, 39.0 us)
Async XLA Ops:
  6.5 6.4 %copy-start = (bf16[512,512]{1,0:T(8,128)(2,1)S(1)}, bf16[512,512]{1,0:T(8,128)(2,1)}, u32[]{:S(2)}) copy-start(bf16[512,512]{1,0:T(8,128)(2,1)} %param.11) | copy-start | bytes 1572868
  15.1 59.6 %copy-start.1 = (s32[4,512]{1,0:T(4,128)S(1)}, s32[4,512]{1,0:T(4,128)}, u32[]{:S(2)}) copy-start(s32[4,512]{1,0:T(4,128)} %param.13) | copy-start | bytes 24580
  16.0 29.3 %all-to-all-start.2 = ((bf16[4,64,8,128]{3,2,0,1:T(8,128)(2,1)}), bf16[4,64,8,128]{3,2,0,1:T(8,128)(2,1)S(1)}, u32[]{:S(2)}, u32[]{:S(2)}) async-start(bf16[4,64,8,128]{3,2,0,1:T(8,128)(2,1)} %copy.44), calls=%async_computation.2 | async-start | bytes 1048576 | tf_op jit(solution)/shard_map/all_to_all | solution.py:92
  45.3 23.4 %all-to-all-start.1 = ((bf16[4,64,8,128]{3,2,0,1:T(8,128)(2,1)}), bf16[4,64,8,128]{3,2,0,1:T(8,128)(2,1)S(1)}, u32[]{:S(2)}, u32[]{:S(2)}) async-start(bf16[4,64,8,128]{3,2,0,1:T(8,128)(2,1)} %copy.42), calls=%async_computation.1 | async-start | bytes 1048576 | tf_op jit(solution)/shard_map/all_to_all | solution.py:91
  68.8 23.4 %all-to-all-start = ((bf16[4,64,8,128]{3,2,0,1:T(8,128)(2,1)}), bf16[4,64,8,128]{3,2,0,1:T(8,128)(2,1)S(1)}, u32[]{:S(2)}, u32[]{:S(2)}) async-start(bf16[4,64,8,128]{3,2,0,1:T(8,128)(2,1)} %copy.40), calls=%async_computation | async-start | bytes 1048576 | tf_op jit(solution)/shard_map/all_to_all | solution.py:90
  74.5 115.8 %all-gather.2.cloned.1.call-start = ((), (), s32[]{:S(2)}) async-start(), calls=%async_computation.4 | async-start | bytes 4259840 | tf_op jit(solution)/shard_map/all_gather | solution.py:124
  94.9 15.1 %collective-permute-start = (bf16[2,4,512,128]{3,2,1,0:T(8,128)(2,1)S(1)}, bf16[2,4,512,128]{3,2,1,0:T(8,128)(2,1)S(1)}, u32[]{:S(2)}, u32[]{:S(2)}) collective-permute-start(bf16[2,4,512,128]{3,2,1,0:T(8,128)(2,1)S(1)} %pad_maximum_fusion.1), channel_id=1, source_target_pairs={{0,8},{8,16},{16,24},{24,32},{32,40},{40,48},{48,56},{56,64},{64,7... | collective-permute-start | bytes 3145736 | tf_op jit(solution)/shard_map/ppermute | solution.py:18
  98.3 16.2 %collective-permute-start.1 = (bf16[2,4,512,128]{3,2,1,0:T(8,128)(2,1)S(1)}, bf16[2,4,512,128]{3,2,1,0:T(8,128)(2,1)}, u32[]{:S(2)}, u32[]{:S(2)}) collective-permute-start(bf16[2,4,512,128]{3,2,1,0:T(8,128)(2,1)S(1)} %pad_maximum_fusion.1), channel_id=1, source_target_pairs={{8,0},{16,8},{24,16},{32,24},{40,32},{48,40},{56,48},{64,56},{72,6... | collective-permute-start | bytes 3145736 | tf_op jit(solution)/shard_map/ppermute | solution.py:20
  100.2 211.7 %all-reduce.3.cloned.1.call-start = ((), (), s32[]{:S(2)}) async-start(), calls=%async_computation.5 | async-start | bytes 8388608 | tf_op jit(solution)/shard_map/psum | solution.py:128
Sparse Core Ops, SparseCore 0:
  100.3 89.9 all-gather.1
  197.0 114.7 all-reduce.2
where the time goes:
time: 322 us; the launch traced here: 321 us
  waiting for transfers between devices  191 us (59%)
  blocking collectives  31.2 us (10%)
  starting transfers between devices  28.6 us (9%)
  local copies, waits for them, and re-layouts  23.8 us (7%)
  matrix products  21.4 us (7%)
  between operations  13.6 us (4%)
  other arithmetic  10.7 us (3%)
    psum x1, waiting for transfers between devices, shards(): lax.psum(partial_value.astype(jnp.bfloat16), 'tp').astype(jnp.float32)  115 us
    all_to_all x1, blocking collectives, shards(): lax.all_to_all(returning, 'seq', split_axis=1, concat_axis=1, tiled=True)  31.2 us
    all_to_all x1, waiting for transfers between devices, shards(): lax.all_to_all(outgoing(2), 'seq', split_axis=1, concat_axis=1, tiled=True)  16.8 us
    all_to_all x1, waiting for transfers between devices, shards(): lax.all_to_all(outgoing(1), 'seq', split_axis=1, concat_axis=1, tiled=True)  16.8 us
    all_to_all x1, waiting for transfers between devices, shards(): lax.all_to_all(outgoing(0), 'seq', split_axis=1, concat_axis=1, tiled=True)  16.1 us
    all_gather x1, waiting for transfers between devices, shards(): lax.all_gather(w_out, 'seq', axis=1, tiled=True)  11.8 us
    all_to_all x1, starting transfers between devices, shards(): lax.all_to_all(outgoing(2), 'seq', split_axis=1, concat_axis=1, tiled=True)  11.6 us
    ppermute x1, waiting for transfers between devices, extended_2(): lax.ppermute(tail, axis, [(i, (i + 1) % count) for i in range(ends)])  9.53 us
  transfers between devices with their start and end apart: 7, of which 7 were waited for; matrix products, arithmetic and copies ran while one was open for 11% of the time, Pallas kernels for 0%

commit v1 on v0

--- a/solution.py
+++ b/solution.py
@@ -121,7 +121,15 @@
     attended = attended.reshape(rows_here, head_count * head_width)
     partial_value = jnp.dot(
         attended,
-        lax.all_gather(w_out, "seq", axis=1, tiled=True),
+        jnp.concatenate(
+            lax.all_to_all(
+                jnp.stack([w_out for _ in range(lax.axis_size("seq"))], axis=0),
+                axis_name="seq",
+                split_axis=0,
+                concat_axis=0,
+            ),
+            axis=1,
+        ),
         preferred_element_type=jnp.float32,
     )
     column_count = partial_value.shape[1] // lax.axis_size("tp")

time: 322 us -> 409 us (1.27)
  waiting for transfers between devices: 191 us -> 274 us
  starting transfers between devices: 28.6 us -> 34.5 us
  blocking collectives: 31.2 us -> 26.8 us
    all_to_all x0 -> x1, waiting for transfers between devices: none -> 93.4 us  [shards(): lax.all_to_all(jnp.stack([w_out for _ in range(lax.axis_size('seq'))], ax...]
    all_gather x1 -> x0, waiting for transfers between devices: 11.8 us -> none  [shards(): lax.all_gather(w_out, 'seq', axis=1, tiled=True)]
    all_to_all x0 -> x1, starting transfers between devices: none -> 5.91 us  [shards(): lax.all_to_all(jnp.stack([w_out for _ in range(lax.axis_size('seq'))], ax...]
    all_to_all x1, blocking collectives: 31.2 us -> 26.8 us  [shards(): lax.all_to_all(returning, 'seq', split_axis=1, concat_axis=1, tiled=True)]
  transfers between devices with their start and end apart: 7 -> 7, of which waited for: 7 -> 7; matrix products, arithmetic and copies ran while one was open for 11% -> 1% of each run, Pallas kernels for 0% -> 0%
where the time goes in v1:
time: 409 us; the launch traced here: 408 us
  waiting for transfers between devices  274 us (67%)
  starting transfers between devices  34.5 us (8%)
  blocking collectives  26.8 us (7%)
  local copies, waits for them, and re-layouts  26.2 us (6%)
  matrix products  21.5 us (5%)
  between operations  13.6 us (3%)
  other arithmetic  10.7 us (3%)
    psum x1, waiting for transfers between devices, shards(): lax.psum(partial_value.astype(jnp.bfloat16), 'tp').astype(jnp.float32)  116 us
    all_to_all x1, waiting for transfers between devices, shards(): lax.all_to_all(jnp.stack([w_out for _ in range(lax.axis_size('seq'))], ax...  93.4 us
    all_to_all x1, blocking collectives, shards(): lax.all_to_all(returning, 'seq', split_axis=1, concat_axis=1, tiled=True)  26.8 us
    all_to_all x1, waiting for transfers between devices, shards(): lax.all_to_all(outgoing(2), 'seq', split_axis=1, concat_axis=1, tiled=True)  16.8 us
    all_to_all x1, waiting for transfers between devices, shards(): lax.all_to_all(outgoing(1), 'seq', split_axis=1, concat_axis=1, tiled=True)  16.8 us
    all_to_all x1, waiting for transfers between devices, shards(): lax.all_to_all(outgoing(0), 'seq', split_axis=1, concat_axis=1, tiled=True)  16.1 us
    all_to_all x1, starting transfers between devices, shards(): lax.all_to_all(outgoing(2), 'seq', split_axis=1, concat_axis=1, tiled=True)  11.6 us
    ppermute x1, waiting for transfers between devices, extended_2(): lax.ppermute(tail, axis, [(i, (i + 1) % count) for i in range(ends)])  9.6 us
  transfers between devices with their start and end apart: 7, of which 7 were waited for; matrix products, arithmetic and copies ran while one was open for 1% of the time, Pallas kernels for 0%

profile of v1, /device:TPU:1, one launch (start us, length us, event | category | flops | bytes accessed | tf_op | source)
XLA Modules:
  0.0 407.7 jit_solution(2999723778482218263)
XLA Ops:
  7.3 1.8 convert_reduce_fusion
  15.9 11.6 %all-to-all-start.2 = ((bf16[4,64,8,128]{3,2,0,1:T(8,128)(2,1)}), bf16[4,64,8,128]{3,2,0,1:T(8,128)(2,1)S(1)}, u32[]{:S(2)}, u32[]{:S(2)}) async-start(bf16[4,64,8,128]{3,2,0,1:T(8,128)(2,1)} %copy.45), calls=%async_computation.2 | async-start | bytes 1048576 | tf_op jit(solution)/shard_map/all_to_all | solution.py:92
  28.4 16.8 %all-to-all-done.2 = bf16[4,64,8,128]{3,2,0,1:T(8,128)(2,1)S(1)} async-done(((bf16[4,64,8,128]{3,2,0,1:T(8,128)(2,1)}), bf16[4,64,8,128]{3,2,0,1:T(8,128)(2,1)S(1)}, u32[]{:S(2)}, u32[]{:S(2)}) %all-to-all-start.2) | async-done | bytes 524320 | tf_op jit(solution)/shard_map/all_to_all | solution.py:92
  45.2 5.7 %all-to-all-start.1 = ((bf16[4,64,8,128]{3,2,0,1:T(8,128)(2,1)}), bf16[4,64,8,128]{3,2,0,1:T(8,128)(2,1)S(1)}, u32[]{:S(2)}, u32[]{:S(2)}) async-start(bf16[4,64,8,128]{3,2,0,1:T(8,128)(2,1)} %copy.43), calls=%async_computation.1 | async-start | bytes 1048576 | tf_op jit(solution)/shard_map/all_to_all | solution.py:91
  51.8 16.8 %all-to-all-done.1 = bf16[4,64,8,128]{3,2,0,1:T(8,128)(2,1)S(1)} async-done(((bf16[4,64,8,128]{3,2,0,1:T(8,128)(2,1)}), bf16[4,64,8,128]{3,2,0,1:T(8,128)(2,1)S(1)}, u32[]{:S(2)}, u32[]{:S(2)}) %all-to-all-start.1) | async-done | bytes 524320 | tf_op jit(solution)/shard_map/all_to_all | solution.py:91
  68.7 5.7 %all-to-all-start = ((bf16[4,64,8,128]{3,2,0,1:T(8,128)(2,1)}), bf16[4,64,8,128]{3,2,0,1:T(8,128)(2,1)S(1)}, u32[]{:S(2)}, u32[]{:S(2)}) async-start(bf16[4,64,8,128]{3,2,0,1:T(8,128)(2,1)} %copy.41), calls=%async_computation | async-start | bytes 1048576 | tf_op jit(solution)/shard_map/all_to_all | solution.py:90
  76.0 16.1 %all-to-all-done = bf16[4,64,8,128]{3,2,0,1:T(8,128)(2,1)S(1)} async-done(((bf16[4,64,8,128]{3,2,0,1:T(8,128)(2,1)}), bf16[4,64,8,128]{3,2,0,1:T(8,128)(2,1)S(1)}, u32[]{:S(2)}, u32[]{:S(2)}) %all-to-all-start) | async-done | bytes 524320 | tf_op jit(solution)/shard_map/all_to_all | solution.py:90
  94.8 3.4 collective-permute-start
  98.2 2.1 collective-permute-start.1
  100.3 9.6 %collective-permute-done = bf16[2,4,512,128]{3,2,1,0:T(8,128)(2,1)S(1)} collective-permute-done((bf16[2,4,512,128]{3,2,1,0:T(8,128)(2,1)S(1)}, bf16[2,4,512,128]{3,2,1,0:T(8,128)(2,1)S(1)}, u32[]{:S(2)}, u32[]{:S(2)}) %collective-permute-start) | collective-permute-done | bytes 1048608 | tf_op jit(solution)/shard_map/ppermute | solution.py:18
  109.9 4.5 %collective-permute-done.1 = bf16[2,4,512,128]{3,2,1,0:T(8,128)(2,1)} collective-permute-done((bf16[2,4,512,128]{3,2,1,0:T(8,128)(2,1)S(1)}, bf16[2,4,512,128]{3,2,1,0:T(8,128)(2,1)}, u32[]{:S(2)}, u32[]{:S(2)}) %collective-permute-start.1) | collective-permute-done | bytes 1048608 | tf_op jit(solution)/shard_map/ppermute | solution.py:20
  117.1 27.3 %while.16 = (s32[]{:T(128)}, bf16[4,512,128]{2,1,0:T(8,128)(2,1)}, s32[4,2,10]{2,1,0:T(2,128)}, bf16[4,512,128]{2,1,0:T(8,128)(2,1)}, bf16[4,1536,128]{2,1,0:T(8...) while((s32[]{:T(128)}, bf16[4,512,128]{2,1,0:T(8,128)(2,1)}, ...), condition=%wide.region_5.6_spmd, body=%wide.region_2.5_spmd.sunk | while | flops 509283360 | bytes 7096867 | solution.py:110
  121.8 1.4 fusion.66
  128.7 1.4 fusion.66
  135.5 1.4 fusion.66
  142.3 1.4 fusion.66
  144.4 1.9 fusion.35
  146.4 26.8 %all_to_all.25 = bf16[4,64,8,128]{3,2,0,1:T(8,128)(2,1)S(1)} all-to-all(bf16[4,64,8,128]{3,2,0,1:T(8,128)(2,1)S(1)} %copy.48), channel_id=1, replica_groups=mesh['seq'=64,'tp'=8] {'seq'}, dimensions={1} | all-to-all | bytes 1048576 | tf_op jit(solution)/shard_map/all_to_all | solution.py:115
  173.1 2.5 stack.11
  175.6 5.9 %all-to-all-start.4 = ((bf16[64,512,64]{1,2,0:T(8,128)(2,1)}), bf16[64,512,64]{1,2,0:T(8,128)(2,1)}, u32[]{:S(2)}, u32[]{:S(2)}) async-start(bf16[64,512,64]{1,2,0:T(8,128)(2,1)} %stack.11), calls=%async_computation.4 | async-start | bytes 8388608 | tf_op jit(solution)/shard_map/all_to_all | solution.py:125
  182.5 93.4 %all-to-all-done.4 = bf16[64,512,64]{1,2,0:T(8,128)(2,1)} async-done(((bf16[64,512,64]{1,2,0:T(8,128)(2,1)}), bf16[64,512,64]{1,2,0:T(8,128)(2,1)}, u32[]{:S(2)}, u32[]{:S(2)}) %all-to-all-start.4) | async-done | bytes 4194336 | tf_op jit(solution)/shard_map/all_to_all | solution.py:125
  276.0 6.6 %convolution_convert_fusion = bf16[512,4096]{1,0:T(8,128)(2,1)} fusion(bf16[512,512]{0,1:T(8,128)(2,1)S(1)} %bitcast.115, bf16[512,4096]{0,1:T(8,128)(2,1)} %bitcast.23), kind=kOutput, calls=%fused_computation.26 | convolution fusion | flops 2149580800 | bytes 8912896 | tf_op jit(solution)/shard_map/dot_general | solution.py:122
  282.6 116.5 %all-reduce.3.cloned.1.call-done = bf16[512,4096]{1,0:T(8,128)(2,1)} async-done(((bf16[512,4096]{1,0:T(8,128)(2,1)}), bf16[512,4096]{1,0:T(8,128)(2,1)}) %all-reduce.3.cloned.1.call-update) | async-done | bytes 4194320 | tf_op jit(solution)/shard_map/psum | solution.py:136
  399.0 1.9 convert_convert_fusion
  (120 shorter events, 41.3 us)
Async XLA Ops:
  6.5 6.4 %copy-start = (bf16[512,512]{1,0:T(8,128)(2,1)S(1)}, bf16[512,512]{1,0:T(8,128)(2,1)}, u32[]{:S(2)}) copy-start(bf16[512,512]{1,0:T(8,128)(2,1)} %param.11) | copy-start | bytes 1572868
  15.0 59.5 %copy-start.2 = (s32[4,512]{1,0:T(4,128)S(1)}, s32[4,512]{1,0:T(4,128)}, u32[]{:S(2)}) copy-start(s32[4,512]{1,0:T(4,128)} %param.13) | copy-start | bytes 24580
  15.9 29.3 %all-to-all-start.2 = ((bf16[4,64,8,128]{3,2,0,1:T(8,128)(2,1)}), bf16[4,64,8,128]{3,2,0,1:T(8,128)(2,1)S(1)}, u32[]{:S(2)}, u32[]{:S(2)}) async-start(bf16[4,64,8,128]{3,2,0,1:T(8,128)(2,1)} %copy.45), calls=%async_computation.2 | async-start | bytes 1048576 | tf_op jit(solution)/shard_map/all_to_all | solution.py:92
  45.2 23.4 %all-to-all-start.1 = ((bf16[4,64,8,128]{3,2,0,1:T(8,128)(2,1)}), bf16[4,64,8,128]{3,2,0,1:T(8,128)(2,1)S(1)}, u32[]{:S(2)}, u32[]{:S(2)}) async-start(bf16[4,64,8,128]{3,2,0,1:T(8,128)(2,1)} %copy.43), calls=%async_computation.1 | async-start | bytes 1048576 | tf_op jit(solution)/shard_map/all_to_all | solution.py:91
  68.7 23.4 %all-to-all-start = ((bf16[4,64,8,128]{3,2,0,1:T(8,128)(2,1)}), bf16[4,64,8,128]{3,2,0,1:T(8,128)(2,1)S(1)}, u32[]{:S(2)}, u32[]{:S(2)}) async-start(bf16[4,64,8,128]{3,2,0,1:T(8,128)(2,1)} %copy.41), calls=%async_computation | async-start | bytes 1048576 | tf_op jit(solution)/shard_map/all_to_all | solution.py:90
  94.8 15.1 %collective-permute-start = (bf16[2,4,512,128]{3,2,1,0:T(8,128)(2,1)S(1)}, bf16[2,4,512,128]{3,2,1,0:T(8,128)(2,1)S(1)}, u32[]{:S(2)}, u32[]{:S(2)}) collective-permute-start(bf16[2,4,512,128]{3,2,1,0:T(8,128)(2,1)S(1)} %pad_maximum_fusion.1), channel_id=1, source_target_pairs={{0,8},{8,16},{16,24},{24,32},{32,40},{40,48},{48,56},{56,64},{64,7... | collective-permute-start | bytes 3145736 | tf_op jit(solution)/shard_map/ppermute | solution.py:18
  98.2 16.2 %collective-permute-start.1 = (bf16[2,4,512,128]{3,2,1,0:T(8,128)(2,1)S(1)}, bf16[2,4,512,128]{3,2,1,0:T(8,128)(2,1)}, u32[]{:S(2)}, u32[]{:S(2)}) collective-permute-start(bf16[2,4,512,128]{3,2,1,0:T(8,128)(2,1)S(1)} %pad_maximum_fusion.1), channel_id=1, source_target_pairs={{8,0},{16,8},{24,16},{32,24},{40,32},{48,40},{56,48},{64,56},{72,6... | collective-permute-start | bytes 3145736 | tf_op jit(solution)/shard_map/ppermute | solution.py:20
  144.4 28.8 %copy-start.1 = (bf16[512,64]{0,1:T(8,128)(2,1)S(1)}, bf16[512,64]{0,1:T(8,128)(2,1)}, u32[]{:S(2)}) copy-start(bf16[512,64]{0,1:T(8,128)(2,1)} %param.15) | copy-start | bytes 196612
  175.6 100.3 %all-to-all-start.4 = ((bf16[64,512,64]{1,2,0:T(8,128)(2,1)}), bf16[64,512,64]{1,2,0:T(8,128)(2,1)}, u32[]{:S(2)}, u32[]{:S(2)}) async-start(bf16[64,512,64]{1,2,0:T(8,128)(2,1)} %stack.11), calls=%async_computation.4 | async-start | bytes 8388608 | tf_op jit(solution)/shard_map/all_to_all | solution.py:125
  181.5 217.5 %all-reduce.3.cloned.1.call-start = ((), (), s32[]{:S(2)}) async-start(), calls=%async_computation.5 | async-start | bytes 8388608 | tf_op jit(solution)/shard_map/psum | solution.py:136
Sparse Core Ops, SparseCore 0:
  282.7 116.3 all-reduce.2
